TPU v7x, 32 devices: a whole 2x2x4 slice. The times are simulated.
32 devices in a mesh: replica: 2 (over x), tensor: 16 (over z, y, core).
Axes of the slice: x: 2, y: 2, z: 4, core: 2. Of those that a mesh axis runs over, the one named last changes fastest.
Arguments:
- tokens: bfloat16 [512, 8192], P('replica', 'tensor'), parts along dimension 0, may hold values from -6 to 6
- gate_matrix: bfloat16 [8192, 28672], P(None, 'tensor'), may hold values from -0.0625 to 0.0625
- up_matrix: bfloat16 [8192, 28672], P(None, 'tensor'), may hold values from -0.0625 to 0.0625
- down_matrix: bfloat16 [28672, 8192], P('tensor'), may hold values from -0.046875 to 0.046875
- adapter_shrink_factors: bfloat16 [16, 16, 28672], P('tensor'), may hold values from -0.03125 to 0.03125
- adapter_expand_factors: bfloat16 [16, 16, 8192], P('tensor'), may hold values from -1.5 to 1.5
- request_adapter_ids: int32 [512, 1], P('replica'), parts along dimension 0, may hold values from 0 to 15
- adapter_store_row: int32 [16], replicated, may hold values from 0 to 15, each once
Outputs:
- mixed: bfloat16 [512, 8192], P('replica', 'tensor'), parts along dimension 0
There are 2 independent parts, one for each index of `replica`. A program takes and returns all parts, laid end to end along the dimension named above; an argument that names none is the same for every part. Nothing has to cross between parts.
Inputs may be any that keep to these rules, and one draw needn't show every extreme that they name: `request_adapter_ids`: every one of the 16 adapter ids is named by at least one row. `adapter_store_row`: A permutation: each store row holds exactly one adapter.
All inputs are finite; a program needn't handle non-finite values.
Results may differ from a plain program's by a relative error of at most 0.0051.
Values may be sent and summed in bfloat16 or wider, within the bound.
A program may use at most 256 MiB of HBM per device.

v0:
```python
import jax
import jax.numpy as jnp
from jax import lax
from jax.sharding import PartitionSpec as P

adapter_scale = 2.0


def local(
    tokens,
    gate_matrix,
    up_matrix,
    down_matrix,
    adapter_shrink_factors,
    adapter_expand_factors,
    request_adapter_ids,
    adapter_store_row,
):
    row_count = tokens.shape[0]
    feature_piece = lax.all_gather(tokens, "tensor", axis=1, tiled=True)
    gate_proj = jnp.dot(feature_piece, gate_matrix, preferred_element_type=jnp.float32)
    up_proj = jnp.dot(feature_piece, up_matrix, preferred_element_type=jnp.float32)
    hidden = (jax.nn.silu(gate_proj) * up_proj).astype(jnp.bfloat16)
    shrink_pages, expand_pages = (
        lax.all_to_all(adapter_shrink_factors, "tensor", split_axis=2, concat_axis=0, tiled=True),
        lax.all_to_all(adapter_expand_factors, "tensor", split_axis=2, concat_axis=0, tiled=True),
    )
    store_count = shrink_pages.shape[0]
    rank_size = shrink_pages.shape[1]
    store_row_ids = adapter_store_row[request_adapter_ids[:, 0]]
    selector = (store_row_ids[:, None] == jnp.arange(store_count, dtype=jnp.int32)[None, :]).astype(
        jnp.float32
    )
    flat_shrink = shrink_pages.reshape(store_count * rank_size, shrink_pages.shape[2])
    every_shrink = jnp.dot(hidden, flat_shrink.T, preferred_element_type=jnp.float32).reshape(
        row_count, store_count, rank_size
    )
    shrink_part = jnp.sum(every_shrink * selector[:, :, None], axis=1)
    shrink_product = lax.psum(shrink_part, "tensor")
    spread_shrink = (selector[:, :, None] * shrink_product[:, None, :]).reshape(
        row_count, store_count * rank_size
    )
    flat_expand = expand_pages.reshape(store_count * rank_size, expand_pages.shape[2]).astype(
        jnp.float32
    )
    adapter_delta = jnp.dot(
        spread_shrink,
        flat_expand,
        precision=lax.Precision.HIGHEST,
        preferred_element_type=jnp.float32,
    )
    partial_out = jnp.dot(hidden, down_matrix, preferred_element_type=jnp.float32)
    base_output = lax.psum_scatter(partial_out, "tensor", scatter_dimension=1, tiled=True)
    return (base_output + adapter_scale * adapter_delta).astype(jnp.bfloat16)


def solution(mesh):
    placed = (
        P("replica", "tensor"),
        P(None, "tensor"),
        P(None, "tensor"),
        P("tensor", None),
        P("tensor", None, None),
        P("tensor", None, None),
        P("replica", None),
        P(),
    )
    return jax.shard_map(
        local, mesh=mesh, in_specs=placed, out_specs=P("replica", "tensor"), check_vma=False
    )
```

profile of v0, /device:TPU:0, one launch (start us, length us, event | category | flops | bytes accessed | tf_op | source)
XLA Modules:
  0.0 507.9 jit_solution(13087498800757092802)
XLA Ops:
  6.5 0.0 all-gather.2.cloned.1.call-start
  6.5 0.7 all-gather.2.cloned.1.call-update
  7.3 0.0 reduce-scatter.2.cloned.1.call-start
  7.3 58.2 %all-gather.2.cloned.1.call-done = bf16[256,8192]{1,0:T(8,128)(2,1)} async-done(((bf16[256,512]{1,0:T(8,128)(2,1)}), bf16[256,8192]{1,0:T(8,128)(2,1)}) %all-gather.2.cloned.1.call-update) | async-done | bytes 4194320 | tf_op jit(solution)/shard_map/all_gather | solution.py:20
  65.5 0.0 copy-start.4
  65.5 19.6 %fusion.8 = f32[256,1792]{1,0:T(8,128)S(1)} fusion(bf16[256,8192]{1,0:T(8,128)(2,1)} %all-gather.2.cloned.1.call-done, bf16[8192,1792]{1,0:T(8,128)(2,1)} %param.9), kind=kOutput, calls=%fused_computation.32 | convolution fusion | flops 7516192768 | bytes 35389440 | tf_op jit(solution)/shard_map/dot_general | solution.py:21
  85.1 0.0 copy-done.4
  85.1 13.8 %fusion = bf16[256,1792]{1,0:T(8,128)(2,1)S(1)} fusion(bf16[256,8192]{1,0:T(8,128)(2,1)S(1)} %copy-done.4, bf16[8192,1792]{1,0:T(8,128)(2,1)} %param.10, f32[256,1792]{1,0:T(8,128)S(1)} %fusion.8), kind=kOutput, calls=%fused_computation.1 | convolution fusion | flops 7518945280 | bytes 36306944 | tf_op jit(solution)/shard_map/dot_general | solution.py:22
  98.9 0.0 copy-start.5
  98.9 0.9 copy-done.5
  99.8 15.3 %fusion.9 = f32[256,8192]{1,0:T(8,128)} fusion(bf16[256,1792]{1,0:T(8,128)(2,1)S(1)} %fusion, bf16[1792,8192]{1,0:T(8,128)(2,1)} %param.11), kind=kOutput, calls=%fused_computation.33 | convolution fusion | flops 7516192768 | bytes 38666240 | tf_op jit(solution)/shard_map/dot_general | solution.py:52
  115.1 0.0 copy-start.1
  115.1 0.0 reduce-scatter.2.cloned.1.call-update
  115.2 0.9 copy-done.1
  116.1 6.6 %copy.15 = bf16[1,16,8192]{1,0,2:T(2,128)(2,1)} copy(bf16[1,16,8192]{2,1,0:T(8,128)(2,1)S(1)} %copy-done.1) | data formatting | bytes 524288 | tf_op args[5]
  122.7 0.6 broadcast.146
  123.3 0.0 copy-start
  123.3 45.5 %reduce.19 = bf16[8192,16]{1,0:T(8,128)(2,1)S(1)} reduce(bf16[8192,1,16]{2,1,0:T(2,128)(2,1)} %bitcast.53, bf16[]{:T(256)} %broadcast.146), dimensions={1}, to_apply=%bitcast.40.reduce_sub_computation | reduce | bytes 524290
  168.9 2.8 reshape.126
  171.7 3.8 all-to-all-start.1
  175.4 0.0 copy-done
  175.4 21.9 %copy.12 = bf16[1,16,28672]{1,0,2:T(2,128)(2,1)} copy(bf16[1,16,28672]{2,1,0:T(8,128)(2,1)S(1)} %copy-done) | data formatting | bytes 1835008 | tf_op args[4]
  197.4 157.2 %reduce.18 = bf16[28672,16]{1,0:T(8,128)(2,1)} reduce(bf16[28672,1,16]{2,1,0:T(2,128)(2,1)} %bitcast.51, bf16[]{:T(256)} %broadcast.146), dimensions={1}, to_apply=%bitcast.38.reduce_sub_computation | reduce | bytes 1835010
  354.6 0.0 copy-start.2
  354.6 0.0 copy-start.3
  354.6 10.4 %reshape.124 = bf16[16,2,14336]{2,1,0:T(2,128)(2,1)} reshape(bf16[28672,16]{1,0:T(8,128)(2,1)} %reduce.18) | data formatting | bytes 1835008
  365.0 0.0 all-to-all-done.1
  365.0 5.7 %all-to-all-start = ((bf16[16,2,14336]{2,1,0:T(2,128)(2,1)}), bf16[16,2,14336]{2,1,0:T(2,128)(2,1)S(1)}, u32[]{:S(2)}, u32[]{:S(2)}) async-start(bf16[16,2,14336]{2,1,0:T(2,128)(2,1)} %reshape.124), calls=%async_computation.1 | async-start | bytes 1835008 | tf_op jit(solution)/shard_map/all_to_all | solution.py:25
  370.8 0.0 copy-done.2
  370.8 0.7 fusion.7
  371.5 0.0 copy-done.3
  371.5 4.4 compare_select_fusion.1
  375.9 5.6 %select_select_fusion = s32[256]{0:T(256)S(1)} fusion(pred[256]{0:T(512)(128)(4,1)S(1)} %get-tuple-element.13, pred[256]{0:T(512)(128)(4,1)S(1)} %get-tuple-element.12, pred[256]{0:T(512)(128)(4,1)S(1)} %get-tuple-element.11, pred[256]{0:T(512)(128)(4,1)S(1)} %get-tuple-element.10, pred[256]{0:T(512)(128)(4,1)S(1)} %get-tuple-element.9, ...), kind=kLoop, calls=%fused_computation.30 | loop fusion | flops 2304 | bytes 4388 | tf_op jit(solution)/shard_map/gather | solution.py:30
  381.5 7.7 %reshape.127 = bf16[8192,1,16]{2,1,0:T(2,128)(2,1)} reshape(bf16[16,2,4096]{2,1,0:T(2,128)(2,1)S(1)} %all-to-all-done.1) | data formatting | bytes 524288
  389.2 7.9 %copy.16 = bf16[1,16,8192]{2,1,0:T(8,128)(2,1)S(1)} copy(bf16[1,16,8192]{1,0,2:T(2,128)(2,1)} %bitcast.54) | data formatting | bytes 524288 | tf_op jit(solution)/shard_map/all_to_all | solution.py:26
  397.0 0.1 copy.19
  397.2 0.2 copy.17
  397.3 0.0 all-to-all-done
  397.3 13.0 %reshape.125 = bf16[28672,1,16]{2,1,0:T(2,128)(2,1)} reshape(bf16[16,2,14336]{2,1,0:T(2,128)(2,1)S(1)} %all-to-all-done) | data formatting | bytes 1835008
  410.3 0.0 copy-start.6
  410.3 26.2 %copy.13 = bf16[1,16,28672]{2,1,0:T(8,128)(2,1)S(1)} copy(bf16[1,16,28672]{1,0,2:T(2,128)(2,1)} %bitcast.52) | data formatting | bytes 1835008 | tf_op jit(solution)/shard_map/all_to_all | solution.py:25
  436.5 0.0 copy-done.6
  436.5 0.4 fusion.3
  437.0 61.9 %psum.7 = f32[256,16]{0,1:T(8,128)S(1)} all-reduce(f32[256,16]{0,1:T(8,128)S(1)} %fusion.3), channel_id=1, replica_groups=mesh['replica'=2,'tensor'=16] {'tensor'}, use_global_device_ids=true, to_apply=%region_2.3 | all-reduce | flops 4096 | bytes 32768 | tf_op jit(solution)/shard_map/psum | solution.py:39
  498.9 0.0 reduce-scatter.2.cloned.1.call-done
  498.9 2.2 fusion.2
  (4 shorter events, 0.1 us)
Async XLA Ops:
  6.5 58.9 %all-gather.2.cloned.1.call-start = ((), (), s32[]{:S(2)}) async-start(), calls=%async_computation.3 | async-start | bytes 4456448 | tf_op jit(solution)/shard_map/all_gather | solution.py:20
  7.3 491.6 %reduce-scatter.2.cloned.1.call-start = ((), (), s32[]{:S(2)}) async-start(), calls=%async_computation.4 | async-start | bytes 8912896 | tf_op jit(solution)/shard_map/reduce_scatter | solution.py:53
  65.5 19.6 %copy-start.4 = (bf16[256,8192]{1,0:T(8,128)(2,1)S(1)}, bf16[256,8192]{1,0:T(8,128)(2,1)}, u32[]{:S(2)}) copy-start(bf16[256,8192]{1,0:T(8,128)(2,1)} %all-gather.2.cloned.1.call-done) | copy-start | bytes 12582916
  98.9 0.9 copy-start.5
  115.1 0.9 copy-start.1
  123.3 52.1 %copy-start = (bf16[1,16,28672]{2,1,0:T(8,128)(2,1)S(1)}, bf16[1,16,28672]{2,1,0:T(8,128)(2,1)}, u32[]{:S(2)}) copy-start(bf16[1,16,28672]{2,1,0:T(8,128)(2,1)} %param.12) | copy-start | bytes 2752516
  171.7 193.3 %all-to-all-start.1 = ((bf16[16,2,4096]{2,1,0:T(2,128)(2,1)}), bf16[16,2,4096]{2,1,0:T(2,128)(2,1)S(1)}, u32[]{:S(2)}, u32[]{:S(2)}) async-start(bf16[16,2,4096]{2,1,0:T(2,128)(2,1)} %reshape.126), calls=%async_computation.2 | async-start | bytes 524288 | tf_op jit(solution)/shard_map/all_to_all | solution.py:26
  354.6 16.2 %copy-start.2 = (s32[16]{0:T(128)S(1)}, s32[16]{0:T(128)}, u32[]{:S(2)}) copy-start(s32[16]{0:T(128)} %param.15) | copy-start | bytes 196
  354.6 16.9 %copy-start.3 = (s32[256,1]{0,1:T(1,128)S(1)}, s32[256,1]{0,1:T(1,128)}, u32[]{:S(2)}) copy-start(s32[256,1]{0,1:T(1,128)} %param.14) | copy-start | bytes 3076
  365.0 32.3 %all-to-all-start = ((bf16[16,2,14336]{2,1,0:T(2,128)(2,1)}), bf16[16,2,14336]{2,1,0:T(2,128)(2,1)S(1)}, u32[]{:S(2)}, u32[]{:S(2)}) async-start(bf16[16,2,14336]{2,1,0:T(2,128)(2,1)} %reshape.124), calls=%async_computation.1 | async-start | bytes 1835008 | tf_op jit(solution)/shard_map/all_to_all | solution.py:25
  410.3 26.2 %copy-start.6 = (bf16[256,1792]{1,0:T(8,128)(2,1)S(1)}, bf16[256,1792]{1,0:T(8,128)(2,1)}, u32[]{:S(2)}) copy-start(bf16[256,1792]{1,0:T(8,128)(2,1)} %copy-done.5) | copy-start | bytes 2752516
Sparse Core Ops, SparseCore 0:
  9.5 55.8 all-gather.1
  115.3 105.9 reduce-scatter.1
where the time goes:
time: 509 us; the launch traced here: 508 us
  other arithmetic  213 us (42%)
  local copies, waits for them, and re-layouts  99.9 us (20%)
  blocking collectives  61.9 us (12%)
  waiting for transfers between devices  58.9 us (12%)
  matrix products  51.3 us (10%)
  between operations  13.6 us (3%)
  starting transfers between devices  9.54 us (2%)
    unnamed x2, other arithmetic  203 us
    unnamed x22, local copies, waits for them, and re-layouts  65 us
    psum x1, blocking collectives, local(): shrink_product = lax.psum(shrink_part, 'tensor')  61.9 us
    all_gather x1, waiting for transfers between devices, local(): feature_piece = lax.all_gather(tokens, 'tensor', axis=1, tiled=True)  58.2 us
    all_to_all x1, local copies, waits for them, and re-layouts, local(): lax.all_to_all(adapter_shrink_factors, 'tensor', split_axis=2, concat_axi...  26.2 us
    dot_general x1, matrix products, local(): jnp.dot(feature_piece, gate_matrix, preferred_element_type=jnp.float32)  19.6 us
    dot_general x1, matrix products, local(): jnp.dot(hidden, down_matrix, preferred_element_type=jnp.float32)  15.3 us
    dot_general x1, matrix products, local(): jnp.dot(feature_piece, up_matrix, preferred_element_type=jnp.float32)  13.8 us
  transfers between devices with their start and end apart: 4, of which 1 were waited for; matrix products, arithmetic and copies ran while one was open for 61% of the time, Pallas kernels for 0%

commit v1 on v0

--- a/solution.py
+++ b/solution.py
@@ -1,6 +1,10 @@
+import functools
+
 import jax
 import jax.numpy as jnp
 from jax import lax
+from jax.experimental import pallas as pl
+from jax.experimental.pallas import tpu as pltpu
 from jax.sharding import PartitionSpec as P
 
 adapter_scale = 2.0
@@ -54,6 +58,443 @@
     return (base_output + adapter_scale * adapter_delta).astype(jnp.bfloat16)
 
 
+layers = 4
+group = 16
+weight_slots = 3
+down_slots = 6
+f32 = jnp.float32
+bf16 = jnp.bfloat16
+NT = (((1,), (1,)), ((), ()))
+
+
+def near_first(z, j):
+    low = jnp.where(z == 0, j, jnp.where(j < 2, 1 - j, j))
+    w = 3 - z
+    high = jnp.where(w == 0, j, jnp.where(j < 2, 1 - j, j))
+    return jnp.where(z < 2, low, 3 - high)
+
+
+def fused(
+    tokens, gate, up, down, shrink, expand, ids, store_row, out,
+    tok, gate_w, up_w, down_w, gate_acc, up_acc, hid, pages, expand_pages,
+    core_send, core_recv, keep, y_send, y_recv, z_send, up_recv, dn_recv, sh_send, sh_recv,
+    tok_recv_sem, tok_core_sem, tok_y_sem, tok_up_sem, tok_dn_sem, own_sem,
+    gate_sem, up_sem, down_sem,
+    core_s, core_r, y_s, y_r, z_s, up_r, dn_r,
+    page_s, page_r, exp_s, exp_r, sh_s, sh_r,
+):
+    me = lax.axis_index("tensor")
+    c, y, z = me % 2, (me // 2) % 2, me // 4
+    piece = tokens.shape[1]
+    units = hid.shape[1]
+    rows = tokens.shape[0]
+    rank = shrink.shape[1]
+
+    def dev(z_, y_, c_):
+        return {"tensor": 4 * z_ + 2 * y_ + c_}
+
+    core_dev = dev(z, y, 1 - c)
+    y_dev = dev(z, 1 - y, c)
+    above = dev(jnp.minimum(z + 1, 3), y, c)
+    below = dev(jnp.maximum(z - 1, 0), y, c)
+
+    def remote(src, dst, s, r, device):
+        return pltpu.make_async_remote_copy(
+            src_ref=src, dst_ref=dst, send_sem=s, recv_sem=r,
+            device_id=device, device_id_type=pl.DeviceIdType.MESH)
+
+    def pair_of(step):
+        second = jnp.where(step == 0, 0, jnp.where(step == 7, 1, 1 - step % 2))
+        at = jnp.where(step == 7, 3, jnp.where(step % 2 == 1, (step + 1) // 2, jnp.maximum(step // 2 - 1, 0)))
+        y_ = jnp.where(second == 1, 1 - y, y)
+        return 2 * near_first(z, at) + y_
+
+    def weights(step):
+        slot = step % weight_slots
+        at = pl.ds(pl.multiple_of(pair_of(step) * 2 * piece, 2 * piece), 2 * piece)
+        return (
+            pltpu.make_async_copy(gate.at[at, :], gate_w.at[slot], gate_sem.at[slot]),
+            pltpu.make_async_copy(up.at[at, :], up_w.at[slot], up_sem.at[slot]),
+        )
+
+    def target(q):
+        g, sub = q // 2, q % 2
+        z_ = near_first(z, 3 - g % 4)
+        y_ = jnp.where(g < 4, 1 - y, y)
+        c_ = jnp.where(sub == 0, 1 - c, c)
+        return 4 * z_ + 2 * y_ + c_
+
+    def down_copy(q):
+        slot = q % down_slots
+        at = pl.ds(pl.multiple_of(target(q) * piece, piece), piece)
+        return pltpu.make_async_copy(down.at[:, at], down_w.at[slot], down_sem.at[slot])
+
+    for step in range(weight_slots):
+        for copy in weights(step):
+            copy.start()
+
+    barrier = pltpu.get_barrier_semaphore()
+
+    @pl.loop(1, group)
+    def _(i):
+        pl.semaphore_signal(barrier, inc=1, device_id={"tensor": (me + i) % group}, device_id_type=pl.DeviceIdType.MESH)
+
+    pl.semaphore_wait(barrier, group - 1)
+
+    def block(z_, y_, c_):
+        return tok.at[2 * z_ + y_, :, pl.ds(pl.multiple_of(c_ * piece, piece), piece)]
+
+    def tok_copy(z_, y_, c_, sem, device, src=None):
+        ref = block(z_, y_, c_)
+        t = 4 * z_ + 2 * y_ + c_
+        return remote(ref if src is None else src, ref, sem, tok_recv_sem.at[t], device)
+
+    def to_core(z_, y_, src=None):
+        return tok_copy(z_, y_, c, tok_core_sem.at[2 * z_ + y_], core_dev, src)
+
+    def to_y(z_, src=None):
+        return tok_copy(z_, y, c, tok_y_sem.at[z_], y_dev, src)
+
+    def to_up(z_, src=None):
+        return tok_copy(z_, y, c, tok_up_sem.at[z_], above, src)
+
+    def to_dn(z_, src=None):
+        return tok_copy(z_, y, c, tok_dn_sem.at[z_], below, src)
+
+    def arrived(z_, y_, c_):
+        tok_copy(z_, y_, c_, tok_up_sem.at[0], core_dev).wait_recv()
+
+    @pl.when(z < 3)
+    def _():
+        to_up(z, tokens).start()
+
+    @pl.when(z > 0)
+    def _():
+        to_dn(z, tokens).start()
+
+    to_y(z, tokens).start()
+    to_core(z, y, tokens).start()
+    own = pltpu.make_async_copy(tokens, block(z, y, c), own_sem)
+    own.start()
+    gate_acc[...] = jnp.zeros_like(gate_acc)
+    up_acc[...] = jnp.zeros_like(up_acc)
+
+    def page_copy(i):
+        other = (me + i) % group
+        at = pl.ds(pl.multiple_of(other * units, 128), units)
+        return remote(shrink.at[0, :, at], pages.at[me], page_s.at[i], page_r.at[me], {"tensor": other})
+
+    def exp_copy(i):
+        other = (me + i) % group
+        at = pl.ds(pl.multiple_of(other * piece, piece), piece)
+        return remote(expand.at[0, :, at], expand_pages.at[me], exp_s.at[i], exp_r.at[me], {"tensor": other})
+
+    def page_arrived(i):
+        other = (me + i) % group
+        remote(pages.at[other], pages.at[other], page_s.at[i], page_r.at[other], core_dev).wait_recv()
+
+    def exp_arrived(i):
+        other = (me + i) % group
+        remote(expand_pages.at[other], expand_pages.at[other], exp_s.at[i], exp_r.at[other], core_dev).wait_recv()
+
+    own_pages = pltpu.make_async_copy(
+        shrink.at[0, :, pl.ds(pl.multiple_of(me * units, 128), units)], pages.at[me], page_r.at[me])
+    own_exp = pltpu.make_async_copy(
+        expand.at[0, :, pl.ds(pl.multiple_of(me * piece, piece), piece)], expand_pages.at[me], exp_r.at[me])
+
+    def z_round(k):
+        @pl.when(z - k >= 0)
+        def _():
+            arrived(z - k, y, c)
+
+            @pl.when(z < 3)
+            def _():
+                to_up(z - k).start()
+
+            to_y(z - k).start()
+            to_core(z - k, y).start()
+
+        @pl.when(z + k <= 3)
+        def _():
+            arrived(z + k, y, c)
+
+            @pl.when(z > 0)
+            def _():
+                to_dn(z + k).start()
+
+            to_y(z + k).start()
+            to_core(z + k, y).start()
+
+    def y_round(j):
+        z_ = near_first(z, j)
+        arrived(z_, 1 - y, c)
+        to_core(z_, 1 - y).start()
+
+    @pl.loop(0, 8)
+    def _(step):
+        for at, act in (
+            (0, lambda: own.wait()),
+            (1, lambda: z_round(1)),
+            (2, lambda: y_round(0)),
+            (3, lambda: z_round(2)),
+            (4, lambda: y_round(1)),
+            (5, lambda: z_round(3)),
+            (6, lambda: y_round(2)),
+            (7, lambda: y_round(3)),
+        ):
+            pl.when(step == at)(act)
+
+        @pl.when(step == page_step)
+        def _():
+            own_pages.start()
+            own_exp.start()
+
+            @pl.loop(1, group)
+            def _(i):
+                page_copy(i).start()
+                exp_copy(i).start()
+
+        pair = pair_of(step)
+        arrived(pair // 2, pair % 2, 1 - c)
+        slot = step % weight_slots
+        for copy in weights(step):
+            copy.wait()
+        here = tok[pair]
+        gate_acc[...] += jnp.dot(here, gate_w[slot], preferred_element_type=f32)
+        up_acc[...] += jnp.dot(here, up_w[slot], preferred_element_type=f32)
+
+        @pl.when(step + weight_slots < 8)
+        def _():
+            for copy in weights(step + weight_slots):
+                copy.start()
+
+        @pl.when(step == 7 - weight_slots + 1)
+        def _():
+            for q in range(down_slots):
+                down_copy(q).start()
+
+    gate_val = gate_acc[...]
+    hid[...] = (gate_val / (1.0 + jnp.exp(-gate_val)) * up_acc[...]).astype(bf16)
+
+    def core_copy(g):
+        return remote(core_send.at[g], core_recv.at[g], core_s.at[g], core_r.at[g], core_dev)
+
+    def y_copy(j):
+        return remote(y_send.at[j], y_recv.at[j], y_s.at[j], y_r.at[j], y_dev)
+
+    def chip_sum(g):
+        core_copy(g).wait_recv()
+        total = keep[g] + core_recv[g].astype(f32)
+
+        @pl.when(g < 4)
+        def _():
+            y_send[g % 4] = total.astype(bf16)
+            y_copy(g % 4).start()
+
+        @pl.when(g >= 4)
+        def _():
+            keep[g] = total
+
+    @pl.loop(0, 16)
+    def _(q):
+        g, sub = q // 2, q % 2
+        down_copy(q).wait()
+        part = jnp.dot(hid[...], down_w[q % down_slots], preferred_element_type=f32)
+
+        @pl.when(q + down_slots < 16)
+        def _():
+            down_copy(q + down_slots).start()
+
+        @pl.when(sub == 0)
+        def _():
+            core_send[g] = part.astype(bf16)
+            core_copy(g).start()
+
+            @pl.when(g > 0)
+            def _():
+                chip_sum(jnp.maximum(g - 1, 0))
+
+        @pl.when(sub == 1)
+        def _():
+            keep[g] = part
+
+    chip_sum(jnp.int32(7))
+
+    own_pages.wait()
+    own_exp.wait()
+
+    @pl.loop(1, group)
+    def _(i):
+        page_arrived(i)
+        exp_arrived(i)
+
+    count = store_row.shape[1]
+    hot = (ids[...] == lax.broadcasted_iota(jnp.int32, (rows, count), 1)).astype(f32)
+    slot_row = lax.dot_general(
+        jnp.broadcast_to(store_row[...].astype(f32), (8, count)), hot, NT,
+        preferred_element_type=f32)[:1]
+    store_at = lax.broadcasted_iota(jnp.int32, (group * rank, rows), 0) // rank
+    chosen = store_at.astype(f32) == slot_row
+    every = lax.dot_general(
+        pages[...].reshape(group * rank, units), hid[...], NT, preferred_element_type=f32)
+    mine = jnp.sum(jnp.where(chosen, every, 0.0).reshape(group, rank, rows), axis=0)
+    sh_send[...] = mine
+
+    def sh_copy(i):
+        other = (me + i) % group
+        return remote(sh_send, sh_recv.at[me], sh_s.at[i], sh_r.at[me], {"tensor": other})
+
+    @pl.loop(1, group)
+    def _(i):
+        sh_copy(i).start()
+
+    sh_recv[me] = mine
+
+    def z_copy(z_, upward):
+        if upward:
+            return remote(z_send.at[z_], up_recv.at[z_], z_s.at[z_], up_r.at[z_], above)
+        return remote(z_send.at[z_], dn_recv.at[z_], z_s.at[z_], dn_r.at[z_], below)
+
+    for j in range(3):
+        z_ = near_first(z, 3 - j)
+        y_copy(j).wait_recv()
+        keep[4 + j] += y_recv[j].astype(f32)
+
+        @pl.when(z_ > z)
+        def _():
+            @pl.when(z > 0)
+            def _():
+                z_copy(z_, True).wait_recv()
+                keep[4 + j] += up_recv[z_].astype(f32)
+
+            z_send[z_] = keep[4 + j].astype(bf16)
+            z_copy(z_, True).start()
+
+        @pl.when(z_ < z)
+        def _():
+            @pl.when(z < 3)
+            def _():
+                z_copy(z_, False).wait_recv()
+                keep[4 + j] += dn_recv[z_].astype(f32)
+
+            z_send[z_] = keep[4 + j].astype(bf16)
+            z_copy(z_, False).start()
+
+    @pl.loop(1, group)
+    def _(i):
+        other = (me + i) % group
+        remote(sh_recv.at[other], sh_recv.at[other], sh_s.at[i], sh_r.at[other], core_dev).wait_recv()
+
+    shrink_sum = jnp.sum(sh_recv[...], axis=0)
+    spread = jnp.where(
+        chosen, jnp.broadcast_to(shrink_sum[None], (group, rank, rows)).reshape(group * rank, rows), 0.0).T
+    flat_expand = expand_pages[...].reshape(group * rank, piece)
+    spread_high = spread.astype(bf16)
+    spread_low = (spread - spread_high.astype(f32)).astype(bf16)
+    delta = jnp.dot(spread_high, flat_expand, preferred_element_type=f32) + jnp.dot(
+        spread_low, flat_expand, preferred_element_type=f32)
+    keep[7] += adapter_scale * delta
+    y_copy(3).wait_recv()
+    keep[7] += y_recv[3].astype(f32)
+
+    @pl.when(z > 0)
+    def _():
+        z_copy(z, True).wait_recv()
+        keep[7] += up_recv[z].astype(f32)
+
+    @pl.when(z < 3)
+    def _():
+        z_copy(z, False).wait_recv()
+        keep[7] += dn_recv[z].astype(f32)
+
+    out[...] = keep[7].astype(bf16)
+
+    for z_ in range(layers):
+        for y_ in range(2):
+            to_core(z_, y_).wait_send()
+        to_y(z_).wait_send()
+
+        @pl.when((z < 3) & (z_ <= z))
+        def _():
+            to_up(z_).wait_send()
+
+        @pl.when((z > 0) & (z_ >= z))
+        def _():
+            to_dn(z_).wait_send()
+
+        y_copy(z_).wait_send()
+
+        @pl.when(z_ != z)
+        def _():
+            z_copy(z_, True).wait_send()
+
+    for g in range(8):
+        core_copy(g).wait_send()
+
+    @pl.loop(1, group)
+    def _(i):
+        page_copy(i).wait_send()
+        exp_copy(i).wait_send()
+        sh_copy(i).wait_send()
+
+
+page_step = 5
+
+
+def local_fused(tokens, gate, up, down, shrink, expand, ids, store_row):
+    rows, piece = tokens.shape
+    units = gate.shape[1]
+    rank = shrink.shape[1]
+    vmem, dma = pltpu.VMEM, pltpu.SemaphoreType.DMA
+    return pl.pallas_call(
+        fused,
+        out_shape=jax.ShapeDtypeStruct((rows, piece), bf16),
+        in_specs=[pl.BlockSpec(memory_space=pltpu.VMEM)]
+        + [pl.BlockSpec(memory_space=pl.ANY)] * 5
+        + [pl.BlockSpec(memory_space=pltpu.VMEM)] * 2,
+        out_specs=pl.BlockSpec(memory_space=pltpu.VMEM),
+        scratch_shapes=[
+            vmem((8, rows, 2 * piece), bf16),
+            vmem((weight_slots, 2 * piece, units), bf16),
+            vmem((weight_slots, 2 * piece, units), bf16),
+            vmem((down_slots, units, piece), bf16),
+            vmem((rows, units), f32),
+            vmem((rows, units), f32),
+            vmem((rows, units), bf16),
+            vmem((group, rank, units), bf16),
+            vmem((group, rank, piece), bf16),
+            vmem((8, rows, piece), bf16),
+            vmem((8, rows, piece), bf16),
+            vmem((8, rows, piece), f32),
+            vmem((4, rows, piece), bf16),
+            vmem((4, rows, piece), bf16),
+            vmem((4, rows, piece), bf16),
+            vmem((4, rows, piece), bf16),
+            vmem((4, rows, piece), bf16),
+            vmem((rank, rows), f32),
+            vmem((group, rank, rows), f32),
+            dma((16,)), dma((8,)), dma((4,)), dma((4,)), dma((4,)), dma,
+            dma((weight_slots,)), dma((weight_slots,)), dma((down_slots,)),
+            dma((8,)), dma((8,)), dma((4,)), dma((4,)), dma((4,)), dma((4,)), dma((4,)),
+            dma((16,)), dma((16,)), dma((16,)), dma((16,)), dma((16,)), dma((16,)),
+        ],
+        compiler_params=pltpu.CompilerParams(
+            collective_id=0, has_side_effects=True, vmem_limit_bytes=63 * 2**20),
+        cost_estimate=pl.CostEstimate(
+            flops=6 * rows * 16 * piece * units, bytes_accessed=6 * 16 * piece * units, transcendentals=rows * units),
+    )(tokens, gate, up, down, shrink, expand, ids, store_row.reshape(1, -1))
+
+
+def pick(mesh_size):
+    def run(tokens, gate, *rest):
+        rows, piece = tokens.shape
+        fits = mesh_size == group and rows % 128 == 0 and piece % 128 == 0 and gate.shape[1] % 128 == 0
+        fits = fits and rest[2].shape[0] == 1 and rest[2].shape[1] == 16
+        return (local_fused if fits else local)(tokens, gate, *rest)
+
+    return run
+
+
 def solution(mesh):
     placed = (
         P("replica", "tensor"),
@@ -66,5 +507,5 @@
         P(),
     )
     return jax.shard_map(
-        local, mesh=mesh, in_specs=placed, out_specs=P("replica", "tensor"), check_vma=False
-    )
+        pick(mesh.shape["tensor"]), mesh=mesh, in_specs=placed, out_specs=P("replica", "tensor"), check_vma=False
+    )

time: 509 us -> 89.7 us (0.18)
  other arithmetic: 213 us -> 0 us
  local copies, waits for them, and re-layouts: 99.9 us -> 3.14 us
  Pallas kernels: 0 us -> 86.4 us
  blocking collectives: 61.9 us -> 0 us
  waiting for transfers between devices: 58.9 us -> 0 us
  matrix products: 51.3 us -> 0 us
  between operations: 13.6 us -> 0.01 us
  starting transfers between devices: 9.54 us -> 0 us
    unnamed x2 -> x0, other arithmetic: 203 us -> none
    pallas_call x0 -> x1, Pallas kernels: none -> 86.4 us  [local_fused(): pl.pallas_call(fused, out_shape=jax.ShapeDtypeStruct((rows, piece), bf16)...]
    psum x1 -> x0, blocking collectives: 61.9 us -> none  [local(): shrink_product = lax.psum(shrink_part, 'tensor')]
    unnamed x22 -> x2, local copies, waits for them, and re-layouts: 65 us -> 3.14 us
    all_gather x1 -> x0, waiting for transfers between devices: 58.2 us -> none  [local(): feature_piece = lax.all_gather(tokens, 'tensor', axis=1, tiled=True)]
    dot_general x5 -> x0, matrix products: 51.3 us -> none  [the longest x1 19.6 us: local(): jnp.dot(feature_piece, gate_matrix, preferred_element_type=jnp.float32)]
    all_to_all x4 -> x0, local copies, waits for them, and re-layouts: 34.2 us -> none  [the longest x1 26.2 us: local(): lax.all_to_all(adapter_shrink_factors, 'tensor', split_axis=2, concat_axi...]
    gather x3 -> x0, other arithmetic: 10 us -> none  [local(): store_row_ids = adapter_store_row[request_adapter_ids[:, 0]]]
  transfers between devices with their start and end apart: 4 -> 0, of which waited for: 1 -> 0; matrix products, arithmetic and copies ran while one was open for 61% -> 0% of each run, Pallas kernels for 0% -> 0%
where the time goes in v1:
time: 89.7 us; the launch traced here: 89.5 us
  Pallas kernels  86.4 us (96%)
  local copies, waits for them, and re-layouts  3.14 us (4%)
    pallas_call x1, Pallas kernels, local_fused(): pl.pallas_call(fused, out_shape=jax.ShapeDtypeStruct((rows, piece), bf16)...  86.4 us
    unnamed x2, local copies, waits for them, and re-layouts  3.14 us

profile of v1, /device:TPU:0, one launch (start us, length us, event | category | flops | bytes accessed | tf_op | source)
XLA Modules:
  0.0 89.5 jit_solution(15686585519361160455)
XLA Ops:
  0.0 1.5 %copy.9.ids = s32[256,1]{1,0:T(8,128)} copy(s32[256,1]{0,1:T(1,128)} %param.14) | data formatting | bytes 2048 | tf_op args[6]
  1.5 86.4 %shard_map.82 = bf16[256,512]{1,0:T(8,128)(2,1)} custom-call(bf16[256,512]{1,0:T(8,128)(2,1)} %tokens.1, bf16[8192,1792]{1,0:T(8,128)(2,1)} %gate.1, bf16[8192,1792]{1,0:T(8,128)(2,1)} %up.1, bf16[1792,8192]{1,0:T(8,128)(2,1)} %down.1, bf16[1,16,28672]{2,1,0:T(8,128)(2,1)} %shrink.1, bf16[1,16,8192]{2,1,0:T(8,128)(2,1)} %expand.1, s32[256,1]{1,0:T(8,128)} %copy.9.ids, ...), custom_call_target="tpu_custom_call" | custom-call | flops 22548578304 | bytes 88080384 | tf_op jit(solution)/shard_map/pallas_call | solution.py:449
  87.9 1.7 %copy.11 = bf16[256,512]{1,0:T(8,128)(2,1)} copy(bf16[256,512]{1,0:T(8,128)(2,1)} %shard_map.82) | data formatting | bytes 524288

commit v2 on v1

--- a/solution.py
+++ b/solution.py
@@ -81,7 +81,7 @@
     tok_recv_sem, tok_core_sem, tok_y_sem, tok_up_sem, tok_dn_sem, own_sem,
     gate_sem, up_sem, down_sem,
     core_s, core_r, y_s, y_r, z_s, up_r, dn_r,
-    page_s, page_r, exp_s, exp_r, sh_s, sh_r,
+    page_s, page_r, exp_s, exp_r, sh_s, sh_r, x_s, x_r,
 ):
     me = lax.axis_index("tensor")
     c, y, z = me % 2, (me // 2) % 2, me // 4
@@ -139,110 +139,145 @@
     def _(i):
         pl.semaphore_signal(barrier, inc=1, device_id={"tensor": (me + i) % group}, device_id_type=pl.DeviceIdType.MESH)
 
-    pl.semaphore_wait(barrier, group - 1)
-
-    def block(z_, y_, c_):
-        return tok.at[2 * z_ + y_, :, pl.ds(pl.multiple_of(c_ * piece, piece), piece)]
-
-    def tok_copy(z_, y_, c_, sem, device, src=None):
-        ref = block(z_, y_, c_)
+    pl.semaphore_signal(
+        barrier, inc=1, device_id={"replica": 1 - lax.axis_index("replica")}, device_id_type=pl.DeviceIdType.MESH)
+    pl.semaphore_wait(barrier, group)
+
+    part = rows // 2
+
+    def half(h):
+        return pl.ds(h * part, part)
+
+    def block(z_, y_, c_, h):
+        return tok.at[2 * z_ + y_, half(h), pl.ds(pl.multiple_of(c_ * piece, piece), piece)]
+
+    def tok_copy(z_, y_, c_, h, sem, device, own):
+        ref = block(z_, y_, c_, h)
         t = 4 * z_ + 2 * y_ + c_
-        return remote(ref if src is None else src, ref, sem, tok_recv_sem.at[t], device)
-
-    def to_core(z_, y_, src=None):
-        return tok_copy(z_, y_, c, tok_core_sem.at[2 * z_ + y_], core_dev, src)
-
-    def to_y(z_, src=None):
-        return tok_copy(z_, y, c, tok_y_sem.at[z_], y_dev, src)
-
-    def to_up(z_, src=None):
-        return tok_copy(z_, y, c, tok_up_sem.at[z_], above, src)
-
-    def to_dn(z_, src=None):
-        return tok_copy(z_, y, c, tok_dn_sem.at[z_], below, src)
-
-    def arrived(z_, y_, c_):
-        tok_copy(z_, y_, c_, tok_up_sem.at[0], core_dev).wait_recv()
-
-    @pl.when(z < 3)
-    def _():
-        to_up(z, tokens).start()
-
-    @pl.when(z > 0)
-    def _():
-        to_dn(z, tokens).start()
-
-    to_y(z, tokens).start()
-    to_core(z, y, tokens).start()
-    own = pltpu.make_async_copy(tokens, block(z, y, c), own_sem)
+        return remote(tokens.at[half(h), :] if own else ref, ref, sem, tok_recv_sem.at[2 * t + h], device)
+
+    def to_core(z_, y_, h, own=False):
+        return tok_copy(z_, y_, c, h, tok_core_sem.at[4 * z_ + 2 * y_ + h], core_dev, own)
+
+    def to_y(z_, h, own=False):
+        return tok_copy(z_, y, c, h, tok_y_sem.at[2 * z_ + h], y_dev, own)
+
+    def to_up(z_, h, own=False):
+        return tok_copy(z_, y, c, h, tok_up_sem.at[2 * z_ + h], above, own)
+
+    def to_dn(z_, h, own=False):
+        return tok_copy(z_, y, c, h, tok_dn_sem.at[2 * z_ + h], below, own)
+
+    def arrived(z_, y_, c_, h):
+        tok_copy(z_, y_, c_, h, tok_up_sem.at[0], core_dev, False).wait_recv()
+
+    for h in range(2):
+        @pl.when(z < 3)
+        def _():
+            to_up(z, h, True).start()
+
+        @pl.when(z > 0)
+        def _():
+            to_dn(z, h, True).start()
+
+        to_y(z, h, True).start()
+
+    for h in range(2):
+        to_core(z, y, h, True).start()
+
+    own = pltpu.make_async_copy(
+        tokens, tok.at[2 * z + y, :, pl.ds(pl.multiple_of(c * piece, piece), piece)], own_sem)
     own.start()
     gate_acc[...] = jnp.zeros_like(gate_acc)
     up_acc[...] = jnp.zeros_like(up_acc)
 
+    r = lax.axis_index("replica")
+    x_dev = {"replica": 1 - r}
+    page_width, exp_width = units // 2, piece // 2
+    page_at = pl.ds(pl.multiple_of(r * page_width, 128), page_width)
+    exp_at = pl.ds(pl.multiple_of(r * exp_width, 128), exp_width)
+
+    def page_source(t):
+        return shrink.at[0, :, pl.ds(pl.multiple_of(t * units + r * page_width, 128), page_width)]
+
+    def exp_source(t):
+        return expand.at[0, :, pl.ds(pl.multiple_of(t * piece + r * exp_width, 128), exp_width)]
+
     def page_copy(i):
         other = (me + i) % group
-        at = pl.ds(pl.multiple_of(other * units, 128), units)
-        return remote(shrink.at[0, :, at], pages.at[me], page_s.at[i], page_r.at[me], {"tensor": other})
+        return remote(page_source(other), pages.at[me, :, page_at], page_s.at[i], page_r.at[me], {"tensor": other})
 
     def exp_copy(i):
         other = (me + i) % group
-        at = pl.ds(pl.multiple_of(other * piece, piece), piece)
-        return remote(expand.at[0, :, at], expand_pages.at[me], exp_s.at[i], exp_r.at[me], {"tensor": other})
+        return remote(exp_source(other), expand_pages.at[me, :, exp_at], exp_s.at[i], exp_r.at[me], {"tensor": other})
 
     def page_arrived(i):
         other = (me + i) % group
-        remote(pages.at[other], pages.at[other], page_s.at[i], page_r.at[other], core_dev).wait_recv()
+        ref = pages.at[other, :, page_at]
+        remote(ref, ref, page_s.at[i], page_r.at[other], core_dev).wait_recv()
 
     def exp_arrived(i):
         other = (me + i) % group
-        remote(expand_pages.at[other], expand_pages.at[other], exp_s.at[i], exp_r.at[other], core_dev).wait_recv()
-
-    own_pages = pltpu.make_async_copy(
-        shrink.at[0, :, pl.ds(pl.multiple_of(me * units, 128), units)], pages.at[me], page_r.at[me])
-    own_exp = pltpu.make_async_copy(
-        expand.at[0, :, pl.ds(pl.multiple_of(me * piece, piece), piece)], expand_pages.at[me], exp_r.at[me])
-
-    def z_round(k):
-        @pl.when(z - k >= 0)
-        def _():
-            arrived(z - k, y, c)
+        ref = expand_pages.at[other, :, exp_at]
+        remote(ref, ref, exp_s.at[i], exp_r.at[other], core_dev).wait_recv()
+
+    own_pages = pltpu.make_async_copy(page_source(me), pages.at[me, :, page_at], page_r.at[me])
+    own_exp = pltpu.make_async_copy(exp_source(me), expand_pages.at[me, :, exp_at], exp_r.at[me])
+    x_pages = remote(pages.at[:, :, page_at], pages.at[:, :, page_at], x_s.at[0], x_r.at[0], x_dev)
+    x_exp = remote(expand_pages.at[:, :, exp_at], expand_pages.at[:, :, exp_at], x_s.at[1], x_r.at[1], x_dev)
+
+    def z_round(k, h):
+        def lower():
+            arrived(z - k, y, c, h)
 
             @pl.when(z < 3)
             def _():
-                to_up(z - k).start()
-
-            to_y(z - k).start()
-            to_core(z - k, y).start()
-
-        @pl.when(z + k <= 3)
-        def _():
-            arrived(z + k, y, c)
+                to_up(z - k, h).start()
+
+            to_y(z - k, h).start()
+            to_core(z - k, y, h).start()
+
+        def upper():
+            arrived(z + k, y, c, h)
 
             @pl.when(z > 0)
             def _():
-                to_dn(z + k).start()
-
-            to_y(z + k).start()
-            to_core(z + k, y).start()
-
-    def y_round(j):
+                to_dn(z + k, h).start()
+
+            to_y(z + k, h).start()
+            to_core(z + k, y, h).start()
+
+        pl.when((z >= 2) & (z + k <= 3))(upper)
+        pl.when(z - k >= 0)(lower)
+        pl.when((z < 2) & (z + k <= 3))(upper)
+
+    def y_round(j, h):
         z_ = near_first(z, j)
-        arrived(z_, 1 - y, c)
-        to_core(z_, 1 - y).start()
+        arrived(z_, 1 - y, c, h)
+        to_core(z_, 1 - y, h).start()
 
     @pl.loop(0, 8)
     def _(step):
-        for at, act in (
-            (0, lambda: own.wait()),
-            (1, lambda: z_round(1)),
-            (2, lambda: y_round(0)),
-            (3, lambda: z_round(2)),
-            (4, lambda: y_round(1)),
-            (5, lambda: z_round(3)),
-            (6, lambda: y_round(2)),
-            (7, lambda: y_round(3)),
-        ):
-            pl.when(step == at)(act)
+        @pl.when(step == 0)
+        def _():
+            own.wait()
+
+        @pl.when(step == 1)
+        def _():
+            for h in range(2):
+                z_round(1, h)
+                y_round(0, h)
+
+        for at in range(2, 6):
+            @pl.when(step == at)
+            def _():
+                z_round(at // 2 + 1, at % 2)
+                y_round(at // 2, at % 2)
+
+        for h in range(2):
+            @pl.when(step == 6 + h)
+            def _():
+                y_round(3, h)
 
         @pl.when(step == page_step)
         def _():
@@ -255,7 +290,8 @@
                 exp_copy(i).start()
 
         pair = pair_of(step)
-        arrived(pair // 2, pair % 2, 1 - c)
+        for h in range(2):
+            arrived(pair // 2, pair % 2, 1 - c, h)
         slot = step % weight_slots
         for copy in weights(step):
             copy.wait()
@@ -279,8 +315,8 @@
     def core_copy(g):
         return remote(core_send.at[g], core_recv.at[g], core_s.at[g], core_r.at[g], core_dev)
 
-    def y_copy(j):
-        return remote(y_send.at[j], y_recv.at[j], y_s.at[j], y_r.at[j], y_dev)
+    def y_copy(j, h):
+        return remote(y_send.at[j, half(h), :], y_recv.at[j, half(h), :], y_s.at[2 * j + h], y_r.at[2 * j + h], y_dev)
 
     def chip_sum(g):
         core_copy(g).wait_recv()
@@ -289,7 +325,8 @@
         @pl.when(g < 4)
         def _():
             y_send[g % 4] = total.astype(bf16)
-            y_copy(g % 4).start()
+            for h in range(2):
+                y_copy(g % 4, h).start()
 
         @pl.when(g >= 4)
         def _():
@@ -320,6 +357,43 @@
 
     chip_sum(jnp.int32(7))
 
+    def z_copy(z_, h, upward):
+        at = 2 * z_ + h
+        src = z_send.at[z_, half(h), :]
+        if upward:
+            return remote(src, up_recv.at[z_, half(h), :], z_s.at[at], up_r.at[at], above)
+        return remote(src, dn_recv.at[z_, half(h), :], z_s.at[at], dn_r.at[at], below)
+
+    def add(g, h, ref):
+        keep[g, half(h), :] += ref[half(h), :].astype(f32)
+
+    def z_stage(j, h):
+        z_ = near_first(z, 3 - j)
+        y_copy(j, h).wait_recv()
+        add(4 + j, h, y_recv.at[j])
+
+        @pl.when(z_ > z)
+        def _():
+            @pl.when(z > 0)
+            def _():
+                z_copy(z_, h, True).wait_recv()
+                add(4 + j, h, up_recv.at[z_])
+
+            z_send[z_, half(h), :] = keep[4 + j, half(h), :].astype(bf16)
+            z_copy(z_, h, True).start()
+
+        @pl.when(z_ < z)
+        def _():
+            @pl.when(z < 3)
+            def _():
+                z_copy(z_, h, False).wait_recv()
+                add(4 + j, h, dn_recv.at[z_])
+
+            z_send[z_, half(h), :] = keep[4 + j, half(h), :].astype(bf16)
+            z_copy(z_, h, False).start()
+
+    z_stage(0, 0)
+
     own_pages.wait()
     own_exp.wait()
 
@@ -328,6 +402,13 @@
         page_arrived(i)
         exp_arrived(i)
 
+    x_pages.start()
+    x_exp.start()
+    z_stage(0, 1)
+    z_stage(1, 0)
+    z_stage(1, 1)
+    x_pages.wait_recv()
+    x_exp.wait_recv()
     count = store_row.shape[1]
     hot = (ids[...] == lax.broadcasted_iota(jnp.int32, (rows, count), 1)).astype(f32)
     slot_row = lax.dot_general(
@@ -349,36 +430,8 @@
         sh_copy(i).start()
 
     sh_recv[me] = mine
-
-    def z_copy(z_, upward):
-        if upward:
-            return remote(z_send.at[z_], up_recv.at[z_], z_s.at[z_], up_r.at[z_], above)
-        return remote(z_send.at[z_], dn_recv.at[z_], z_s.at[z_], dn_r.at[z_], below)
-
-    for j in range(3):
-        z_ = near_first(z, 3 - j)
-        y_copy(j).wait_recv()
-        keep[4 + j] += y_recv[j].astype(f32)
-
-        @pl.when(z_ > z)
-        def _():
-            @pl.when(z > 0)
-            def _():
-                z_copy(z_, True).wait_recv()
-                keep[4 + j] += up_recv[z_].astype(f32)
-
-            z_send[z_] = keep[4 + j].astype(bf16)
-            z_copy(z_, True).start()
-
-        @pl.when(z_ < z)
-        def _():
-            @pl.when(z < 3)
-            def _():
-                z_copy(z_, False).wait_recv()
-                keep[4 + j] += dn_recv[z_].astype(f32)
-
-            z_send[z_] = keep[4 + j].astype(bf16)
-            z_copy(z_, False).start()
+    z_stage(2, 0)
+    z_stage(2, 1)
 
     @pl.loop(1, group)
     def _(i):
@@ -394,39 +447,42 @@
     delta = jnp.dot(spread_high, flat_expand, preferred_element_type=f32) + jnp.dot(
         spread_low, flat_expand, preferred_element_type=f32)
     keep[7] += adapter_scale * delta
-    y_copy(3).wait_recv()
-    keep[7] += y_recv[3].astype(f32)
-
-    @pl.when(z > 0)
-    def _():
-        z_copy(z, True).wait_recv()
-        keep[7] += up_recv[z].astype(f32)
-
-    @pl.when(z < 3)
-    def _():
-        z_copy(z, False).wait_recv()
-        keep[7] += dn_recv[z].astype(f32)
-
-    out[...] = keep[7].astype(bf16)
-
+    for h in range(2):
+        @pl.when(z > 0)
+        def _():
+            z_copy(z, h, True).wait_recv()
+            add(7, h, up_recv.at[z])
+
+        @pl.when(z < 3)
+        def _():
+            z_copy(z, h, False).wait_recv()
+            add(7, h, dn_recv.at[z])
+
+    for h in range(2):
+        y_copy(3, h).wait_recv()
+        out[half(h), :] = (keep[7, half(h), :] + y_recv[3, half(h), :].astype(f32)).astype(bf16)
+
+    x_pages.wait_send()
+    x_exp.wait_send()
     for z_ in range(layers):
-        for y_ in range(2):
-            to_core(z_, y_).wait_send()
-        to_y(z_).wait_send()
-
-        @pl.when((z < 3) & (z_ <= z))
-        def _():
-            to_up(z_).wait_send()
-
-        @pl.when((z > 0) & (z_ >= z))
-        def _():
-            to_dn(z_).wait_send()
-
-        y_copy(z_).wait_send()
-
-        @pl.when(z_ != z)
-        def _():
-            z_copy(z_, True).wait_send()
+        for h in range(2):
+            for y_ in range(2):
+                to_core(z_, y_, h).wait_send()
+            to_y(z_, h).wait_send()
+
+            @pl.when((z < 3) & (z_ <= z))
+            def _():
+                to_up(z_, h).wait_send()
+
+            @pl.when((z > 0) & (z_ >= z))
+            def _():
+                to_dn(z_, h).wait_send()
+
+            y_copy(z_, h).wait_send()
+
+            @pl.when(z_ != z)
+            def _():
+                z_copy(z_, h, True).wait_send()
 
     for g in range(8):
         core_copy(g).wait_send()
@@ -438,7 +494,7 @@
         sh_copy(i).wait_send()
 
 
-page_step = 5
+page_step = 7
 
 
 def local_fused(tokens, gate, up, down, shrink, expand, ids, store_row):
@@ -473,10 +529,10 @@
             vmem((4, rows, piece), bf16),
             vmem((rank, rows), f32),
             vmem((group, rank, rows), f32),
-            dma((16,)), dma((8,)), dma((4,)), dma((4,)), dma((4,)), dma,
+            dma((32,)), dma((16,)), dma((8,)), dma((8,)), dma((8,)), dma,
             dma((weight_slots,)), dma((weight_slots,)), dma((down_slots,)),
-            dma((8,)), dma((8,)), dma((4,)), dma((4,)), dma((4,)), dma((4,)), dma((4,)),
-            dma((16,)), dma((16,)), dma((16,)), dma((16,)), dma((16,)), dma((16,)),
+            dma((8,)), dma((8,)), dma((8,)), dma((8,)), dma((8,)), dma((8,)), dma((8,)),
+            dma((16,)), dma((16,)), dma((16,)), dma((16,)), dma((16,)), dma((16,)), dma((2,)), dma((2,)),
         ],
         compiler_params=pltpu.CompilerParams(
             collective_id=0, has_side_effects=True, vmem_limit_bytes=63 * 2**20),
@@ -485,10 +541,10 @@
     )(tokens, gate, up, down, shrink, expand, ids, store_row.reshape(1, -1))
 
 
-def pick(mesh_size):
+def pick(mesh_size, replicas):
     def run(tokens, gate, *rest):
         rows, piece = tokens.shape
-        fits = mesh_size == group and rows % 128 == 0 and piece % 128 == 0 and gate.shape[1] % 128 == 0
+        fits = (mesh_size, replicas) == (group, 2) and rows % 128 == 0 and piece % 256 == 0 and gate.shape[1] % 256 == 0
         fits = fits and rest[2].shape[0] == 1 and rest[2].shape[1] == 16
         return (local_fused if fits else local)(tokens, gate, *rest)
 
@@ -507,5 +563,5 @@
         P(),
     )
     return jax.shard_map(
-        pick(mesh.shape["tensor"]), mesh=mesh, in_specs=placed, out_specs=P("replica", "tensor"), check_vma=False
-    )
+        pick(mesh.shape["tensor"], mesh.shape["replica"]), mesh=mesh, in_specs=placed, out_specs=P("replica", "tensor"), check_vma=False
+    )

time: 89.7 us -> 82.9 us (0.924)
  Pallas kernels: 86.4 us -> 79.5 us
    pallas_call x1, Pallas kernels: 86.4 us -> 79.5 us  [local_fused(): pl.pallas_call(fused, out_shape=jax.ShapeDtypeStruct((rows, piece), bf16)...]
where the time goes in v2:
time: 82.9 us; the launch traced here: 82.7 us
  Pallas kernels  79.5 us (96%)
  local copies, waits for them, and re-layouts  3.14 us (4%)
    pallas_call x1, Pallas kernels, local_fused(): pl.pallas_call(fused, out_shape=jax.ShapeDtypeStruct((rows, piece), bf16)...  79.5 us
    unnamed x2, local copies, waits for them, and re-layouts  3.14 us

profile of v2, /device:TPU:0, one launch (start us, length us, event | category | flops | bytes accessed | tf_op | source)
XLA Modules:
  0.0 82.7 jit_solution(5318824083064274423)
XLA Ops:
  0.0 1.5 %copy.9.ids = s32[256,1]{1,0:T(8,128)} copy(s32[256,1]{0,1:T(1,128)} %param.14) | data formatting | bytes 2048 | tf_op args[6]
  1.5 79.5 %shard_map.82 = bf16[256,512]{1,0:T(8,128)(2,1)} custom-call(bf16[256,512]{1,0:T(8,128)(2,1)} %tokens.1, bf16[8192,1792]{1,0:T(8,128)(2,1)} %gate.1, bf16[8192,1792]{1,0:T(8,128)(2,1)} %up.1, bf16[1792,8192]{1,0:T(8,128)(2,1)} %down.1, bf16[1,16,28672]{2,1,0:T(8,128)(2,1)} %shrink.1, bf16[1,16,8192]{2,1,0:T(8,128)(2,1)} %expand.1, s32[256,1]{1,0:T(8,128)} %copy.9.ids, ...), custom_call_target="tpu_custom_call" | custom-call | flops 22548578304 | bytes 88080384 | tf_op jit(solution)/shard_map/pallas_call | solution.py:505
  81.0 1.7 %copy.11 = bf16[256,512]{1,0:T(8,128)(2,1)} copy(bf16[256,512]{1,0:T(8,128)(2,1)} %shard_map.82) | data formatting | bytes 524288

commit v3 on v2

--- a/solution.py
+++ b/solution.py
@@ -141,6 +141,8 @@
 
     pl.semaphore_signal(
         barrier, inc=1, device_id={"replica": 1 - lax.axis_index("replica")}, device_id_type=pl.DeviceIdType.MESH)
+    gate_acc[...] = jnp.zeros_like(gate_acc)
+    up_acc[...] = jnp.zeros_like(up_acc)
     pl.semaphore_wait(barrier, group)
 
     part = rows // 2
@@ -188,8 +190,6 @@
     own = pltpu.make_async_copy(
         tokens, tok.at[2 * z + y, :, pl.ds(pl.multiple_of(c * piece, piece), piece)], own_sem)
     own.start()
-    gate_acc[...] = jnp.zeros_like(gate_acc)
-    up_acc[...] = jnp.zeros_like(up_acc)
 
     r = lax.axis_index("replica")
     x_dev = {"replica": 1 - r}
@@ -410,10 +410,9 @@
     x_pages.wait_recv()
     x_exp.wait_recv()
     count = store_row.shape[1]
-    hot = (ids[...] == lax.broadcasted_iota(jnp.int32, (rows, count), 1)).astype(f32)
-    slot_row = lax.dot_general(
-        jnp.broadcast_to(store_row[...].astype(f32), (8, count)), hot, NT,
-        preferred_element_type=f32)[:1]
+    hot = (ids[...] == lax.broadcasted_iota(jnp.int32, (count, rows), 0)).astype(f32)
+    slot_row = jnp.dot(
+        jnp.broadcast_to(store_row[...].astype(f32), (8, count)), hot, preferred_element_type=f32)[:1]
     store_at = lax.broadcasted_iota(jnp.int32, (group * rank, rows), 0) // rank
     chosen = store_at.astype(f32) == slot_row
     every = lax.dot_general(
@@ -538,7 +537,7 @@
             collective_id=0, has_side_effects=True, vmem_limit_bytes=63 * 2**20),
         cost_estimate=pl.CostEstimate(
             flops=6 * rows * 16 * piece * units, bytes_accessed=6 * 16 * piece * units, transcendentals=rows * units),
-    )(tokens, gate, up, down, shrink, expand, ids, store_row.reshape(1, -1))
+    )(tokens, gate, up, down, shrink, expand, ids.reshape(1, -1), store_row.reshape(1, -1))
 
 
 def pick(mesh_size, replicas):

time: 82.9 us -> 81.3 us (0.981)
  local copies, waits for them, and re-layouts: 3.14 us -> 1.67 us
    unnamed x2 -> x1, local copies, waits for them, and re-layouts: 3.14 us -> 1.67 us
where the time goes in v3:
time: 81.3 us; the launch traced here: 81.1 us
  Pallas kernels  79.4 us (98%)
  local copies, waits for them, and re-layouts  1.67 us (2%)
    pallas_call x1, Pallas kernels, local_fused(): pl.pallas_call(fused, out_shape=jax.ShapeDtypeStruct((rows, piece), bf16)...  79.4 us
    unnamed x1, local copies, waits for them, and re-layouts  1.67 us

profile of v3, /device:TPU:0, one launch (start us, length us, event | category | flops | bytes accessed | tf_op | source)
XLA Modules:
  0.0 81.1 jit_solution(4427170932392113438)
XLA Ops:
  0.0 79.4 %shard_map.82 = bf16[256,512]{1,0:T(8,128)(2,1)} custom-call(bf16[256,512]{1,0:T(8,128)(2,1)} %tokens.1, bf16[8192,1792]{1,0:T(8,128)(2,1)} %gate.1, bf16[8192,1792]{1,0:T(8,128)(2,1)} %up.1, bf16[1792,8192]{1,0:T(8,128)(2,1)} %down.1, bf16[1,16,28672]{2,1,0:T(8,128)(2,1)} %shrink.1, bf16[1,16,8192]{2,1,0:T(8,128)(2,1)} %expand.1, s32[1,256]{1,0:T(1,128)} %bitcast.2, ...), custom_call_target="tpu_custom_call" | custom-call | flops 22548578304 | bytes 88080384 | tf_op jit(solution)/shard_map/pallas_call | solution.py:504
  79.4 1.7 %copy.10 = bf16[256,512]{1,0:T(8,128)(2,1)} copy(bf16[256,512]{1,0:T(8,128)(2,1)} %shard_map.82) | data formatting | bytes 524288
